TPU v7x, 32 devices: a whole 2x2x4 slice. The times are simulated.
32 devices in a mesh: parts: 2 (over y), blk: 4 (over z), sub: 4 (over x, core).
Axes of the slice: x: 2, y: 2, z: 4, core: 2. Of those that a mesh axis runs over, the one named last changes fastest.
Arguments:
- readings: float32 [2, 24576, 256], P(None, ('parts', 'blk', 'sub')), parts along dimension 1, may hold values from -6 to 6
- coverage: int32 [2, 24576, 256], P(None, ('parts', 'blk', 'sub')), parts along dimension 1, may hold values 0 or 1
- pixel_factors: float32 [24576, 256], P(('parts', 'blk', 'sub')), parts along dimension 0, may hold values from -1.5 to 1.5
- date_factors: float32 [2048, 256], P(('parts', 'blk', 'sub')), parts along dimension 0, may hold values from -1.5 to 1.5
Outputs:
- pixel_out: float32 [24576, 256], P(('parts', 'blk', 'sub')), parts along dimension 0
- date_out: float32 [2048, 256], P(('parts', 'blk', 'sub')), parts along dimension 0
There are 2 independent parts, one for each index of `parts`. A program takes and returns all parts, laid end to end along the dimension named above; each array names one. Nothing has to cross between parts.
All inputs are finite; a program needn't handle non-finite values. No bound on the sum of `coverage` on one device may be relied on, other than what follows from the above.
Results may differ from a plain program's by a relative error of at most 0.0001.
Values sent between devices are 32-bit elements; how exact they have to be, the bound alone decides.
A program may use at most 64 MiB of HBM per device.

v0:
```python
import jax
import jax.numpy as jnp
from jax import lax
from jax.sharding import PartitionSpec as P

STRATA = 2


step_size = 0.05
ridge = 0.1
epsilon = 1e-06


def from_behind(value, axis, steps):
    count = lax.axis_size(axis)
    pairs = [(source, (source + steps) % count) for source in range(count)]
    return lax.ppermute(value, axis, pairs)


def local_terms(values, weights, strip, block):
    hp = lax.Precision.HIGHEST
    predicted = lax.dot_general(strip, block, (((1,), (1,)), ((), ())), precision=hp)
    errors = weights * (values - predicted)
    pixel_grad = -jnp.dot(errors, block, precision=hp) + ridge * strip
    date_part = -lax.dot_general(errors, strip, (((0,), (0,)), ((), ())), precision=hp)
    return (pixel_grad, date_part)


def on_device(readings, coverage, pixel_factors, date_factors):
    strip = pixel_factors
    share_rows = date_factors.shape[0]
    groups = lax.axis_size("sub")
    block_rows = share_rows * groups
    pixel_count = strip.shape[0] * groups * strip.shape[1]
    date_count = block_rows * strip.shape[1]
    share = date_factors
    for stratum in range(STRATA):
        block = lax.all_gather(share, "sub", axis=0, tiled=True)
        values = readings[stratum]
        weights = coverage[stratum].astype(jnp.float32)
        pixel_grad, date_part = local_terms(values, weights, strip, block)
        own_part = lax.psum_scatter(date_part, "sub", scatter_dimension=0, tiled=True)
        date_grad = own_part + ridge * share
        pixel_sq, date_sq = lax.psum(
            (jnp.sum(pixel_grad * pixel_grad), jnp.sum(date_grad * date_grad)), "sub"
        )
        strip = strip - step_size * pixel_grad / jnp.sqrt(pixel_sq / pixel_count + epsilon)
        share = share - step_size * date_grad / jnp.sqrt(date_sq / date_count + epsilon)
        share = from_behind(share, "blk", 1)
    return (strip, share)


def solution(mesh):
    in_specs = (
        P(None, ("parts", "blk", "sub"), None),
        P(None, ("parts", "blk", "sub"), None),
        P(("parts", "blk", "sub"), None),
        P(("parts", "blk", "sub"), None),
    )
    out_specs = (P(("parts", "blk", "sub"), None), P(("parts", "blk", "sub"), None))
    return jax.shard_map(
        on_device, mesh=mesh, in_specs=in_specs, out_specs=out_specs, check_vma=False
    )
```

profile of v0, /device:TPU:0, one launch (start us, length us, event | category | flops | bytes accessed | tf_op | source)
XLA Modules:
  0.0 110.2 jit_solution(7786691914013596123)
XLA Ops:
  7.2 0.0 reduce-scatter.3.cloned.1.call-start
  7.2 7.4 %all_gather.6 = f32[256,256]{1,0:T(8,128)S(1)} all-gather(f32[64,256]{1,0:T(8,128)} %param.7), channel_id=1, replica_groups=mesh['parts'=2,'blk'=4,'sub'=4] {'sub'}, dimensions={0}, use_global_device_ids=true | all-gather | bytes 327680 | tf_op jit(solution)/shard_map/all_gather | solution.py:38
  14.6 0.0 copy-start
  14.6 2.5 %fusion.3 = f32[768,256]{1,0:T(8,128)S(1)} fusion(f32[768,256]{1,0:T(8,128)} %param.6, f32[256,256]{1,0:T(8,128)S(1)} %all_gather.6, f32[2,768,256]{2,1,0:T(8,128)} %param.4, s32[2,768,256]{2,1,0:T(8,128)} %param.5), kind=kOutput, calls=%fused_computation.7 | convolution fusion | flops 604569600 | bytes 3407872 | tf_op jit(solution)/shard_map/dot_general | solution.py:22
  17.1 0.0 copy-done
  17.1 2.1 %convolution_negate_fusion.3 = f32[256,256]{1,0:T(8,128)} fusion(f32[768,256]{1,0:T(8,128)S(1)} %fusion.3, f32[768,256]{1,0:T(8,128)S(1)} %copy-done), kind=kOutput, calls=%fused_computation.9 | convolution fusion | flops 604045312 | bytes 1835008 | tf_op jit(solution)/shard_map/dot_general | solution.py:25
  19.2 0.0 copy-start.1
  19.3 0.0 reduce-scatter.3.cloned.1.call-update
  19.3 0.0 reduce-scatter.5.cloned.1.call-start
  19.3 1.4 %multiply_reduce_fusion.1 = (f32[]{:T(128)}, f32[768,256]{1,0:T(8,128)S(1)}) fusion(f32[768,256]{1,0:T(8,128)S(1)} %copy-done, f32[768,256]{1,0:T(8,128)S(1)} %fusion.3, f32[256,256]{1,0:T(8,128)S(1)} %all_gather.6), kind=kOutput, calls=%fused_computation.13 | convolution fusion | flops 604962816 | bytes 2621444 | tf_op jit(solution)/shard_map/dot_general | solution.py:24
  20.7 20.0 %reduce-scatter.3.cloned.1.call-done = f32[64,256]{1,0:T(8,128)} async-done(((f32[256,256]{1,0:T(8,128)}), f32[64,256]{1,0:T(8,128)}) %reduce-scatter.3.cloned.1.call-update) | async-done | bytes 65552 | tf_op jit(solution)/shard_map/reduce_scatter | solution.py:42
  40.8 0.0 copy-done.1
  40.8 1.5 %multiply_reduce_fusion.3 = f32[]{:T(128)} fusion(f32[64,256]{1,0:T(8,128)} %reduce-scatter.3.cloned.1.call-done, f32[64,256]{1,0:T(8,128)S(1)} %copy-done.1), kind=kLoop, calls=%fused_computation.18 | loop fusion | flops 65535 | bytes 131076 | tf_op jit(solution)/shard_map/reduce_sum | solution.py:45
  42.3 6.4 %all-reduce.1 = (f32[]{:T(128)}, f32[]{:T(128)}) all-reduce(f32[]{:T(128)} %get-tuple-element.6, f32[]{:T(128)} %multiply_reduce_fusion.3), channel_id=1, replica_groups=mesh['parts'=2,'blk'=4,'sub'=4] {'sub'}, use_global_device_ids=true, to_apply=%region_1.0 | all-reduce | flops 2 | bytes 16 | tf_op jit(solution)/shard_map/psum | solution.py:44
  50.0 0.9 divide_subtract_fusion.3
  50.9 1.7 %collective-permute-start = (f32[64,256]{1,0:T(8,128)S(1)}, f32[64,256]{1,0:T(8,128)S(1)}, u32[]{:S(2)}, u32[]{:S(2)}) collective-permute-start(f32[64,256]{1,0:T(8,128)S(1)} %divide_subtract_fusion.3), channel_id=1, source_target_pairs={{0,4},{4,8},{8,12},{12,0},{1,5},{5,9},{9,13},{13,1},{2,6},{6,10},{... | collective-permute-start | bytes 196616 | tf_op jit(solution)/shard_map/ppermute | solution.py:17
  52.6 0.1 divide_subtract_fusion.1
  52.7 4.3 %collective-permute-done = f32[64,256]{1,0:T(8,128)S(1)} collective-permute-done((f32[64,256]{1,0:T(8,128)S(1)}, f32[64,256]{1,0:T(8,128)S(1)}, u32[]{:S(2)}, u32[]{:S(2)}) %collective-permute-start) | collective-permute-done | bytes 65568 | tf_op jit(solution)/shard_map/ppermute | solution.py:17
  57.0 5.9 %all_gather.7 = f32[256,256]{1,0:T(8,128)S(1)} all-gather(f32[64,256]{1,0:T(8,128)S(1)} %collective-permute-done), channel_id=1, replica_groups=mesh['parts'=2,'blk'=4,'sub'=4] {'sub'}, dimensions={0}, use_global_device_ids=true | all-gather | bytes 327680 | tf_op jit(solution)/shard_map/all_gather | solution.py:38
  62.8 2.2 %fusion.2 = f32[768,256]{1,0:T(8,128)S(1)} fusion(f32[768,256]{1,0:T(8,128)S(1)} %divide_subtract_fusion.1, f32[256,256]{1,0:T(8,128)S(1)} %all_gather.7, f32[2,768,256]{2,1,0:T(8,128)} %param.4, s32[2,768,256]{2,1,0:T(8,128)} %param.5), kind=kOutput, calls=%fused_computation.5 | convolution fusion | flops 604569600 | bytes 3407872 | tf_op jit(solution)/shard_map/dot_general | solution.py:22
  65.0 2.1 %convolution_negate_fusion.2 = f32[256,256]{1,0:T(8,128)} fusion(f32[768,256]{1,0:T(8,128)S(1)} %fusion.2, f32[768,256]{1,0:T(8,128)S(1)} %divide_subtract_fusion.1), kind=kOutput, calls=%fused_computation.8 | convolution fusion | flops 604045312 | bytes 1835008 | tf_op jit(solution)/shard_map/dot_general | solution.py:25
  67.2 0.0 reduce-scatter.5.cloned.1.call-update
  67.2 1.4 %multiply_reduce_fusion = (f32[]{:T(128)}, f32[768,256]{1,0:T(8,128)S(1)}) fusion(f32[768,256]{1,0:T(8,128)S(1)} %divide_subtract_fusion.1, f32[768,256]{1,0:T(8,128)S(1)} %fusion.2, f32[256,256]{1,0:T(8,128)S(1)} %all_gather.7), kind=kOutput, calls=%fused_computation.11 | convolution fusion | flops 604962816 | bytes 2621444 | tf_op jit(solution)/shard_map/dot_general | solution.py:24
  68.6 18.0 %reduce-scatter.5.cloned.1.call-done = f32[64,256]{1,0:T(8,128)} async-done(((f32[256,256]{1,0:T(8,128)}), f32[64,256]{1,0:T(8,128)}) %reduce-scatter.5.cloned.1.call-update) | async-done | bytes 65552 | tf_op jit(solution)/shard_map/reduce_scatter | solution.py:42
  86.6 1.5 %multiply_reduce_fusion.2 = f32[]{:T(128)} fusion(f32[64,256]{1,0:T(8,128)} %reduce-scatter.5.cloned.1.call-done, f32[64,256]{1,0:T(8,128)S(1)} %collective-permute-done), kind=kLoop, calls=%fused_computation.15 | loop fusion | flops 65535 | bytes 131076 | tf_op jit(solution)/shard_map/reduce_sum | solution.py:45
  88.0 6.4 %all-reduce = (f32[]{:T(128)}, f32[]{:T(128)}) all-reduce(f32[]{:T(128)} %get-tuple-element.8, f32[]{:T(128)} %multiply_reduce_fusion.2), channel_id=1, replica_groups=mesh['parts'=2,'blk'=4,'sub'=4] {'sub'}, use_global_device_ids=true, to_apply=%region_6.0 | all-reduce | flops 2 | bytes 16 | tf_op jit(solution)/shard_map/psum | solution.py:44
  95.8 0.9 divide_subtract_fusion.2
  96.6 1.7 %collective-permute-start.1 = (f32[64,256]{1,0:T(8,128)S(1)}, f32[64,256]{1,0:T(8,128)S(1)}, u32[]{:S(2)}, u32[]{:S(2)}) collective-permute-start(f32[64,256]{1,0:T(8,128)S(1)} %divide_subtract_fusion.2), channel_id=1, source_target_pairs={{0,4},{4,8},{8,12},{12,0},{1,5},{5,9},{9,13},{13,1},{2,6},{6,10},{... | collective-permute-start | bytes 196616 | tf_op jit(solution)/shard_map/ppermute | solution.py:17
  98.4 1.0 divide_subtract_fusion
  99.3 3.4 %collective-permute-done.1 = f32[64,256]{1,0:T(8,128)S(1)} collective-permute-done((f32[64,256]{1,0:T(8,128)S(1)}, f32[64,256]{1,0:T(8,128)S(1)}, u32[]{:S(2)}, u32[]{:S(2)}) %collective-permute-start.1) | collective-permute-done | bytes 65568 | tf_op jit(solution)/shard_map/ppermute | solution.py:17
  102.8 0.6 copy.7
Async XLA Ops:
  7.2 33.6 %reduce-scatter.3.cloned.1.call-start = ((), (), s32[]{:S(2)}) async-start(), calls=%async_computation.2 | async-start | bytes 327680 | tf_op jit(solution)/shard_map/reduce_scatter | solution.py:42
  14.6 2.5 %copy-start = (f32[768,256]{1,0:T(8,128)S(1)}, f32[768,256]{1,0:T(8,128)}, u32[]{:S(2)}) copy-start(f32[768,256]{1,0:T(8,128)} %param.6) | copy-start | bytes 2359300
  19.2 21.5 %copy-start.1 = (f32[64,256]{1,0:T(8,128)S(1)}, f32[64,256]{1,0:T(8,128)}, u32[]{:S(2)}) copy-start(f32[64,256]{1,0:T(8,128)} %param.7) | copy-start | bytes 196612
  19.3 67.3 %reduce-scatter.5.cloned.1.call-start = ((), (), s32[]{:S(2)}) async-start(), calls=%async_computation.3 | async-start | bytes 327680 | tf_op jit(solution)/shard_map/reduce_scatter | solution.py:42
  50.9 6.1 %collective-permute-start = (f32[64,256]{1,0:T(8,128)S(1)}, f32[64,256]{1,0:T(8,128)S(1)}, u32[]{:S(2)}, u32[]{:S(2)}) collective-permute-start(f32[64,256]{1,0:T(8,128)S(1)} %divide_subtract_fusion.3), channel_id=1, source_target_pairs={{0,4},{4,8},{8,12},{12,0},{1,5},{5,9},{9,13},{13,1},{2,6},{6,10},{... | collective-permute-start | bytes 196616 | tf_op jit(solution)/shard_map/ppermute | solution.py:17
  96.6 6.1 %collective-permute-start.1 = (f32[64,256]{1,0:T(8,128)S(1)}, f32[64,256]{1,0:T(8,128)S(1)}, u32[]{:S(2)}, u32[]{:S(2)}) collective-permute-start(f32[64,256]{1,0:T(8,128)S(1)} %divide_subtract_fusion.2), channel_id=1, source_target_pairs={{0,4},{4,8},{8,12},{12,0},{1,5},{5,9},{9,13},{13,1},{2,6},{6,10},{... | collective-permute-start | bytes 196616 | tf_op jit(solution)/shard_map/ppermute | solution.py:17
Sparse Core Ops, SparseCore 0:
  19.4 21.3 reduce-scatter.2
  67.3 19.2 reduce-scatter.4
where the time goes:
time: 111 us; the launch traced here: 110 us
  waiting for transfers between devices  45.7 us (41%)
  blocking collectives  26 us (23%)
  between operations  16.8 us (15%)
  matrix products  11.7 us (11%)
  other arithmetic  5.73 us (5%)
  starting transfers between devices  3.54 us (3%)
    reduce_scatter x2, waiting for transfers between devices, on_device(): lax.psum_scatter(date_part, 'sub', scatter_dimension=0, tiled=True)  38 us
    all_gather x2, blocking collectives, on_device(): block = lax.all_gather(share, 'sub', axis=0, tiled=True)  13.3 us
    psum x2, blocking collectives, on_device(): lax.psum((jnp.sum(pixel_grad * pixel_grad), jnp.sum(date_grad * date_grad...  12.7 us
    ppermute x2, waiting for transfers between devices, from_behind(): return lax.ppermute(value, axis, pairs)  7.69 us
    dot_general x2, matrix products, local_terms(): lax.dot_general(strip, block, (((1,), (1,)), ((), ())), precision=hp)  4.68 us
    dot_general x2, matrix products, local_terms(): lax.dot_general(errors, strip, (((0,), (0,)), ((), ())), precision=hp)  4.24 us
    ppermute x2, starting transfers between devices, from_behind(): return lax.ppermute(value, axis, pairs)  3.45 us
    reduce_sum x2, other arithmetic, on_device(): jnp.sum(date_grad * date_grad)  2.92 us
  transfers between devices with their start and end apart: 4, of which 4 were waited for; matrix products, arithmetic and copies ran while one was open for 4% of the time, Pallas kernels for 0%

commit v1 on v0

v1 whole, which is shorter than its diff:
```python
import functools

import jax
import jax.numpy as jnp
from jax import lax
from jax.experimental import pallas as pl
from jax.experimental.pallas import tpu as pltpu
from jax.sharding import PartitionSpec as P

STRATA = 2
MESH = pl.DeviceIdType.MESH

step_size = 0.05
ridge = 0.1
epsilon = 1e-06

F32 = jnp.float32
BF16 = jnp.bfloat16


def split(value):
    high = value.astype(BF16)
    return high, (value - high.astype(F32)).astype(BF16)


def dot3(a, b, dims=((1,), (0,))):
    dot = functools.partial(
        lax.dot_general, dimension_numbers=(dims, ((), ())), preferred_element_type=F32
    )
    return dot(a[0], b[0]) + (dot(a[0], b[1]) + dot(a[1], b[0]))


def folded_squares(value):
    rows, columns = value.shape
    squares = value * value
    total = jnp.sum(squares.reshape(rows // 8, 8, columns), axis=0)
    return sum(total[:, i : i + 128] for i in range(0, columns, 128))


def whole_sum(value):
    return jnp.sum(jnp.sum(value, axis=0, keepdims=True), axis=1, keepdims=True)


def kernel(
    strips, groups, pieces, x_hbm, m_hbm, w_hbm, h_hbm, w_out, h_out,
    xs, ms, w, gw, wh, wl, eh, el, th, tl,
    h0, hprev, h1, hh, hl, gath, part, arecv, bsend, brecv, red, crecv, hrecv,
    psq, precv, dsq, drecv, wres, hres,
    lsem, ssem, rsem,
):
    z, s = lax.axis_index("blk"), lax.axis_index("sub")
    chips = groups // 2
    x, c = lax.div(s, 2), lax.rem(s, 2)
    rows, rank = w.shape
    share_rows = h_hbm.shape[0]
    piece = share_rows // pieces
    tile = 256 if rows % 256 == 0 else rows
    tiles = rows // tile
    znext, zprev = lax.rem(z + 1, strips), lax.rem(z + strips - 1, strips)
    mate = {"blk": z, "sub": 2 * x + 1 - c}
    ahead = {"blk": znext, "sub": s}
    pixel_count = rows * groups * rank
    date_count = share_rows * groups * rank

    def chip(step):
        return lax.rem(x + step + chips, chips)

    def cut(k):
        return pl.ds(k * piece, piece)

    used = [0]
    sent = []

    def slots(n):
        first = used[0]
        used[0] += n
        return first

    def send(src, dst, slot, device):
        copy = pltpu.make_async_remote_copy(
            src_ref=src, dst_ref=dst, send_sem=ssem.at[slot], recv_sem=rsem.at[slot],
            device_id=device, device_id_type=MESH,
        )
        copy.start()
        sent.append(copy)

    def arrived(dst, slot):
        pltpu.make_async_remote_copy(
            src_ref=dst, dst_ref=dst, send_sem=ssem.at[slot], recv_sem=rsem.at[slot],
            device_id=mate, device_id_type=MESH,
        ).wait_recv()

    loads = [
        pltpu.make_async_copy(h_hbm, h0.at[s], lsem.at[0]),
        pltpu.make_async_copy(w_hbm, w, lsem.at[1]),
        pltpu.make_async_copy(x_hbm.at[0], xs.at[0], lsem.at[2]),
        pltpu.make_async_copy(m_hbm.at[0], ms.at[0], lsem.at[3]),
        pltpu.make_async_copy(x_hbm.at[1], xs.at[1], lsem.at[4]),
        pltpu.make_async_copy(m_hbm.at[1], ms.at[1], lsem.at[5]),
    ]
    for load in loads:
        load.start()

    barrier = pltpu.get_barrier_semaphore()
    for step in range(1, groups):
        pl.semaphore_signal(
            barrier, inc=1, device_id={"blk": z, "sub": lax.rem(s + step, groups)},
            device_id_type=MESH,
        )
    for step in range(groups):
        for where in (znext, zprev):
            pl.semaphore_signal(
                barrier, inc=1, device_id={"blk": where, "sub": lax.rem(s + step, groups)},
                device_id_type=MESH,
            )
    pl.semaphore_wait(barrier, 3 * groups - 1)

    ag_x = slots(chips * pieces)
    ag_mate = slots(1)
    ag_fwd = slots(chips * pieces)
    hp_z = slots(chips)
    hp_mate = slots(chips)
    a_slot = [slots(chips) for _ in range(STRATA)]
    b_slot = [slots(chips * pieces) for _ in range(STRATA)]
    p_slot = [slots(groups) for _ in range(STRATA)]
    c_slot = [slots(pieces) for _ in range(STRATA)]
    d_slot = slots(chips * pieces)
    e_slot = slots(chips * pieces)
    h1_slot = slots(1)
    q_slot = slots(groups)

    for k in range(pieces):
        for i in range(1, chips):
            send(
                h_hbm.at[cut(k)], h0.at[s, cut(k)], ag_x + i * pieces + k,
                {"blk": z, "sub": 2 * chip(i) + c},
            )
    send(h_hbm, h0.at[s], ag_mate, mate)
    loads[0].wait()
    loads[1].wait()
    for b in range(tiles):
        at = pl.ds(b * tile, tile)
        wh[at, :], wl[at, :] = split(w[at, :])
    for k in range(pieces):
        for i in range(1, chips):
            share = 2 * chip(-i) + c
            arrived(h0.at[share, cut(k)], ag_x + i * pieces + k)
            send(h0.at[share, cut(k)], h0.at[share, cut(k)], ag_fwd + i * pieces + k, mate)
    arrived(h0.at[2 * x + 1 - c], ag_mate)
    for i in range(chips):
        share = 2 * chip(i) + c
        send(h0.at[share], hprev.at[share], hp_z + i, ahead)
    for k in range(pieces):
        for i in range(1, chips):
            arrived(h0.at[2 * chip(-i) + 1 - c, cut(k)], ag_fwd + i * pieces + k)

    def errors(t, held):
        hh[...], hl[...] = split(held[...].reshape(groups * share_rows, rank))
        loads[2 + 2 * t].wait()
        loads[3 + 2 * t].wait()
        for b in range(tiles):
            at = pl.ds(b * tile, tile)
            predicted = dot3((wh[at, :], wl[at, :]), (hh[...], hl[...]), ((1,), (1,)))
            e = ms[t, at, :].astype(F32) * (xs[t, at, :] - predicted)
            eh[at, :], el[at, :] = split(e)
            th[:, at], tl[:, at] = split(e.T)

    def date_sums(t, held):
        for i in [*range(1, chips), 0]:
            to = chip(i)
            at = pl.ds(pl.multiple_of(to * 2 * share_rows, 2 * share_rows), 2 * share_rows)
            sums = dot3((th[at, :], tl[at, :]), (wh[...], wl[...]))
            part[t, pl.ds(2 * to, 2)] = -sums.reshape(2, share_rows, rank)
            send(part.at[t, 2 * to + 1 - c], arecv.at[t, to], a_slot[t] + i, mate)
        for i in [*range(1, chips), 0]:
            to = chip(i)
            arrived(arecv.at[t, to], a_slot[t] + i)
            if i:
                for k in range(pieces):
                    bsend[t, i, cut(k)] = part[t, 2 * to + c, cut(k)] + arecv[t, to, cut(k)]
                    send(
                        bsend.at[t, i, cut(k)], brecv.at[t, i, cut(k)],
                        b_slot[t] + i * pieces + k, {"blk": z, "sub": 2 * to + c},
                    )
            else:
                red[t] = part[t, s] + arecv[t, to] + ridge * held[s]

    def pixel_grads(t):
        squares = jnp.zeros((8, 128), F32)
        for b in range(tiles):
            at = pl.ds(b * tile, tile)
            grad = ridge * w[at, :] - dot3((eh[at, :], el[at, :]), (hh[...], hl[...]))
            gw[at, :] = grad
            squares += folded_squares(grad)
        psq[t] = squares
        for step in range(1, groups):
            send(
                psq.at[t], precv.at[t, step], p_slot[t] + step,
                {"blk": z, "sub": lax.rem(s + step, groups)},
            )

    def date_shares(t, landing):
        for k in range(pieces):
            value = red[t, cut(k)]
            for i in range(1, chips):
                arrived(brecv.at[t, i, cut(k)], b_slot[t] + i * pieces + k)
                value += brecv[t, i, cut(k)]
            red[t, cut(k)] = value
            send(red.at[t, cut(k)], landing.at[cut(k)], c_slot[t] + k, ahead)

    def pixel_scale(t):
        total = psq[t]
        for step in range(1, groups):
            arrived(precv.at[t, step], p_slot[t] + step)
            total += precv[t, step]
        return step_size / jnp.sqrt(whole_sum(total) / pixel_count + epsilon)

    errors(0, h0)
    date_sums(0, h0)
    pixel_grads(0)
    date_shares(0, gath.at[s])
    for i in range(chips):
        share = 2 * chip(i) + c
        arrived(hprev.at[share], hp_z + i)
        send(hprev.at[share], hprev.at[share], hp_mate + i, mate)
    scale = pixel_scale(0)
    for b in range(tiles):
        at = pl.ds(b * tile, tile)
        value = w[at, :] - scale * gw[at, :]
        w[at, :] = value
        wh[at, :], wl[at, :] = split(value)

    for k in range(pieces):
        arrived(gath.at[s, cut(k)], c_slot[0] + k)
        for i in range(1, chips):
            send(
                gath.at[s, cut(k)], gath.at[s, cut(k)], d_slot + i * pieces + k,
                {"blk": z, "sub": 2 * chip(i) + c},
            )
        send(gath.at[s, cut(k)], gath.at[s, cut(k)], e_slot + k, mate)
    for k in range(pieces):
        for i in range(1, chips):
            share = 2 * chip(-i) + c
            arrived(gath.at[share, cut(k)], d_slot + i * pieces + k)
            send(gath.at[share, cut(k)], gath.at[share, cut(k)], e_slot + i * pieces + k, mate)
    for i in range(chips):
        arrived(hprev.at[2 * chip(i) + 1 - c], hp_mate + i)
    for k in range(pieces):
        for i in range(chips):
            arrived(gath.at[2 * chip(-i) + 1 - c, cut(k)], e_slot + i * pieces + k)
    grads = gath[...].reshape(groups * share_rows, rank)
    scale = step_size / jnp.sqrt(whole_sum(folded_squares(grads)) / date_count + epsilon)
    h1[...] = hprev[...] - scale.reshape(1, 1, 1) * gath[...]
    send(h1.at[s], hrecv, h1_slot, ahead)

    errors(1, h1)
    date_sums(1, h1)
    pixel_grads(1)
    date_shares(1, crecv)
    dsq[...] = folded_squares(red[1])
    for step in range(groups):
        send(
            dsq, drecv.at[step], q_slot + step,
            {"blk": znext, "sub": lax.rem(s + step, groups)},
        )
    scale = pixel_scale(1)
    for b in range(tiles):
        at = pl.ds(b * tile, tile)
        wres[at, :] = w[at, :] - scale * gw[at, :]
    w_store = pltpu.make_async_copy(wres, w_out, lsem.at[6])
    w_store.start()
    total = jnp.zeros((8, 128), F32)
    for step in range(groups):
        arrived(drecv.at[step], q_slot + step)
        total += drecv[step]
    scale = step_size / jnp.sqrt(whole_sum(total) / date_count + epsilon)
    arrived(hrecv, h1_slot)
    for k in range(pieces):
        arrived(crecv.at[cut(k)], c_slot[1] + k)
    hres[...] = hrecv[...] - scale * crecv[...]
    h_store = pltpu.make_async_copy(hres, h_out, lsem.at[7])
    h_store.start()
    for copy in sent:
        copy.wait_send()
    w_store.wait()
    h_store.wait()
    assert used[0] <= ssem.shape[0]


def on_device(strips, groups, readings, coverage, pixel_factors, date_factors):
    rows, rank = pixel_factors.shape
    share_rows = date_factors.shape[0]
    dates = share_rows * groups
    chips = groups // 2
    pieces = 2
    vmem = pltpu.VMEM
    block = vmem((groups, share_rows, rank), F32)
    by_chip = vmem((STRATA, chips, share_rows, rank), F32)
    share = vmem((share_rows, rank), F32)
    strip = vmem((rows, rank), F32)
    slots = 10 + 12 * chips * pieces + 12 * chips
    scratch = [
        vmem((STRATA, rows, dates), F32), vmem((STRATA, rows, dates), jnp.int32),
        strip, strip,
        vmem((rows, rank), BF16), vmem((rows, rank), BF16),
        vmem((rows, dates), BF16), vmem((rows, dates), BF16),
        vmem((dates, rows), BF16), vmem((dates, rows), BF16),
        block, block, block,
        vmem((dates, rank), BF16), vmem((dates, rank), BF16),
        block,
        vmem((STRATA, groups, share_rows, rank), F32),
        by_chip, by_chip, by_chip,
        vmem((STRATA, share_rows, rank), F32),
        share, share,
        vmem((STRATA, 8, 128), F32), vmem((STRATA, groups, 8, 128), F32),
        vmem((8, 128), F32), vmem((groups, 8, 128), F32),
        strip, share,
        pltpu.SemaphoreType.DMA((8,)),
        pltpu.SemaphoreType.DMA((slots,)),
        pltpu.SemaphoreType.DMA((slots,)),
    ]
    anywhere = pl.BlockSpec(memory_space=pl.ANY)
    return pl.pallas_call(
        functools.partial(kernel, strips, groups, pieces),
        out_shape=(
            jax.ShapeDtypeStruct((rows, rank), F32),
            jax.ShapeDtypeStruct((share_rows, rank), F32),
        ),
        in_specs=[pl.BlockSpec(memory_space=pltpu.HBM)] * 4,
        out_specs=(anywhere, anywhere),
        scratch_shapes=scratch,
        compiler_params=pltpu.CompilerParams(
            collective_id=0, has_side_effects=True, vmem_limit_bytes=48 * 1024 * 1024
        ),
    )(readings, coverage, pixel_factors, date_factors)


def solution(mesh):
    in_specs = (
        P(None, ("parts", "blk", "sub"), None),
        P(None, ("parts", "blk", "sub"), None),
        P(("parts", "blk", "sub"), None),
        P(("parts", "blk", "sub"), None),
    )
    out_specs = (P(("parts", "blk", "sub"), None), P(("parts", "blk", "sub"), None))
    return jax.shard_map(
        functools.partial(on_device, mesh.shape["blk"], mesh.shape["sub"]),
        mesh=mesh, in_specs=in_specs, out_specs=out_specs, check_vma=False,
    )
```

time: 111 us -> 40.5 us (0.36)
  waiting for transfers between devices: 45.7 us -> 0 us
  Pallas kernels: 0 us -> 33.3 us
  blocking collectives: 26 us -> 0 us
  between operations: 16.8 us -> 0.65 us
  matrix products: 11.7 us -> 0 us
  other arithmetic: 5.73 us -> 0 us
  local copies, waits for them, and re-layouts: 0.64 us -> 6.29 us
  starting transfers between devices: 3.54 us -> 0 us
    reduce_scatter x2 -> x0, waiting for transfers between devices: 38 us -> none  [on_device(): lax.psum_scatter(date_part, 'sub', scatter_dimension=0, tiled=True)]
    pallas_call x0 -> x1, Pallas kernels: none -> 33.3 us  [on_device(): pl.pallas_call(functools.partial(kernel, strips, groups, pieces), out_sha...]
    all_gather x2 -> x0, blocking collectives: 13.3 us -> none  [on_device(): block = lax.all_gather(share, 'sub', axis=0, tiled=True)]
    psum x2 -> x0, blocking collectives: 12.7 us -> none  [on_device(): lax.psum((jnp.sum(pixel_grad * pixel_grad), jnp.sum(date_grad * date_grad...]
    dot_general x6 -> x0, matrix products: 11.7 us -> none  [the longest x2 4.68 us: local_terms(): lax.dot_general(strip, block, (((1,), (1,)), ((), ())), precision=hp)]
    ppermute x2 -> x0, waiting for transfers between devices: 7.69 us -> none  [from_behind(): return lax.ppermute(value, axis, pairs)]
    unnamed x5 -> x10, local copies, waits for them, and re-layouts: 0.64 us -> 6.29 us
    ppermute x2 -> x0, starting transfers between devices: 3.45 us -> none  [from_behind(): return lax.ppermute(value, axis, pairs)]
  transfers between devices with their start and end apart: 4 -> 0, of which waited for: 4 -> 0; matrix products, arithmetic and copies ran while one was open for 4% -> 0% of each run, Pallas kernels for 0% -> 0%
where the time goes in v1:
time: 40.5 us; the launch traced here: 40.3 us
  Pallas kernels  33.3 us (82%)
  local copies, waits for them, and re-layouts  6.29 us (16%)
  between operations  0.65 us (2%)
    pallas_call x1, Pallas kernels, on_device(): pl.pallas_call(functools.partial(kernel, strips, groups, pieces), out_sha...  33.3 us
    unnamed x10, local copies, waits for them, and re-layouts  6.29 us

profile of v1, /device:TPU:0, one launch (start us, length us, event | category | flops | bytes accessed | tf_op | source)
XLA Modules:
  0.0 40.3 jit_solution(18284723944971092177)
XLA Ops:
  0.6 0.0 copy-start
  0.6 1.4 %copy-done = f32[2,768,256]{2,1,0:T(8,128)S(1)} copy-done((f32[2,768,256]{2,1,0:T(8,128)S(1)}, f32[2,768,256]{2,1,0:T(8,128)}, u32[]{:S(2)}) %copy-start) | copy-done | bytes 1572888
  2.0 0.0 copy-start.1
  2.0 1.4 %copy-done.1 = s32[2,768,256]{2,1,0:T(8,128)S(1)} copy-done((s32[2,768,256]{2,1,0:T(8,128)S(1)}, s32[2,768,256]{2,1,0:T(8,128)}, u32[]{:S(2)}) %copy-start.1) | copy-done | bytes 1572888
  3.4 0.0 copy-start.2
  3.5 1.1 %copy-done.2 = f32[768,256]{1,0:T(8,128)S(1)} copy-done((f32[768,256]{1,0:T(8,128)S(1)}, f32[768,256]{1,0:T(8,128)}, u32[]{:S(2)}) %copy-start.2) | copy-done | bytes 786456
  4.6 0.0 copy-start.3
  4.6 0.8 %copy-done.3 = f32[64,256]{1,0:T(8,128)S(1)} copy-done((f32[64,256]{1,0:T(8,128)S(1)}, f32[64,256]{1,0:T(8,128)}, u32[]{:S(2)}) %copy-start.3) | copy-done | bytes 65560
  5.4 33.3 %shard_map.59 = (f32[768,256]{1,0:T(8,128)S(1)}, f32[64,256]{1,0:T(8,128)S(1)}) custom-call(f32[2,768,256]{2,1,0:T(8,128)S(1)} %copy-done, s32[2,768,256]{2,1,0:T(8,128)S(1)} %copy-done.1, f32[768,256]{1,0:T(8,128)S(1)} %copy-done.2, f32[64,256]{1,0:T(8,128)S(1)} %copy-done.3), custom_call_target="tpu_custom_call" | custom-call | tf_op jit(solution)/shard_map/pallas_call | solution.py:323
  38.8 0.9 %copy.8 = f32[768,256]{1,0:T(8,128)} copy(f32[768,256]{1,0:T(8,128)S(1)} %get-tuple-element.4) | data formatting | bytes 1572864
  39.7 0.6 %copy.9 = f32[64,256]{1,0:T(8,128)} copy(f32[64,256]{1,0:T(8,128)S(1)} %get-tuple-element.5) | data formatting | bytes 131072
Async XLA Ops:
  0.6 1.4 %copy-start = (f32[2,768,256]{2,1,0:T(8,128)S(1)}, f32[2,768,256]{2,1,0:T(8,128)}, u32[]{:S(2)}) copy-start(f32[2,768,256]{2,1,0:T(8,128)} %x_hbm.1) | copy-start | bytes 4718596
  2.0 1.4 %copy-start.1 = (s32[2,768,256]{2,1,0:T(8,128)S(1)}, s32[2,768,256]{2,1,0:T(8,128)}, u32[]{:S(2)}) copy-start(s32[2,768,256]{2,1,0:T(8,128)} %m_hbm.1) | copy-start | bytes 4718596
  3.4 1.1 %copy-start.2 = (f32[768,256]{1,0:T(8,128)S(1)}, f32[768,256]{1,0:T(8,128)}, u32[]{:S(2)}) copy-start(f32[768,256]{1,0:T(8,128)} %w_hbm.1) | copy-start | bytes 2359300
  4.6 0.8 %copy-start.3 = (f32[64,256]{1,0:T(8,128)S(1)}, f32[64,256]{1,0:T(8,128)}, u32[]{:S(2)}) copy-start(f32[64,256]{1,0:T(8,128)} %h_hbm.1) | copy-start | bytes 196612

commit v2 on v1

v2 whole, which is shorter than its diff:
```python
import functools

import jax
import jax.numpy as jnp
from jax import lax
from jax.experimental import pallas as pl
from jax.experimental.pallas import tpu as pltpu
from jax.sharding import PartitionSpec as P

STRATA = 2
MESH = pl.DeviceIdType.MESH

step_size = 0.05
ridge = 0.1
epsilon = 1e-06

F32 = jnp.float32
BF16 = jnp.bfloat16


def split(value):
    high = value.astype(BF16)
    return high, (value - high.astype(F32)).astype(BF16)


def dot3(a, b, dims=((1,), (0,))):
    dot = functools.partial(
        lax.dot_general, dimension_numbers=(dims, ((), ())), preferred_element_type=F32
    )
    return dot(a[0], b[0]) + (dot(a[0], b[1]) + dot(a[1], b[0]))


def folded_squares(value):
    rows, columns = value.shape
    squares = value * value
    total = jnp.sum(squares.reshape(rows // 8, 8, columns), axis=0)
    return sum(total[:, i : i + 128] for i in range(0, columns, 128))


def whole_sum(value):
    return jnp.sum(jnp.sum(value, axis=0, keepdims=True), axis=1, keepdims=True)


def kernel(
    strips, groups, x_hbm, m_hbm, w_hbm, h_hbm, w_out, h_out,
    xs, ms, w, gw, wh, wl, eh, el, th, tl,
    h0, hprev, h1, hh, hl, gath, part, arecv, red, crecv, hrecv,
    psq, precv, dsq, drecv, wres, hres,
    lsem, ssem, rsem,
):
    z, s = lax.axis_index("blk"), lax.axis_index("sub")
    chips = groups // 2
    x, c = lax.div(s, 2), lax.rem(s, 2)
    rows, rank = w.shape
    share_rows = h_hbm.shape[0]
    tile = 256 if rows % 256 == 0 else rows
    tiles = rows // tile
    znext, zprev = lax.rem(z + 1, strips), lax.rem(z + strips - 1, strips)
    mate = {"blk": z, "sub": 2 * x + 1 - c}
    ahead = {"blk": znext, "sub": s}
    pixel_count = rows * groups * rank
    date_count = share_rows * groups * rank

    def chip(step):
        return lax.rem(x + step + chips, chips)

    def peer(step):
        return lax.rem(s + step + groups, groups)

    used = [0]
    sent = []

    def slots(n):
        first = used[0]
        used[0] += n
        return first

    def send(src, dst, slot, device):
        copy = pltpu.make_async_remote_copy(
            src_ref=src, dst_ref=dst, send_sem=ssem.at[slot], recv_sem=rsem.at[slot],
            device_id=device, device_id_type=MESH,
        )
        copy.start()
        sent.append(copy)

    def arrived(dst, slot):
        pltpu.make_async_remote_copy(
            src_ref=dst, dst_ref=dst, send_sem=ssem.at[slot], recv_sem=rsem.at[slot],
            device_id=mate, device_id_type=MESH,
        ).wait_recv()

    loads = [
        pltpu.make_async_copy(h_hbm, h0.at[s], lsem.at[0]),
        pltpu.make_async_copy(w_hbm, w, lsem.at[1]),
        pltpu.make_async_copy(x_hbm.at[0], xs.at[0], lsem.at[2]),
        pltpu.make_async_copy(m_hbm.at[0], ms.at[0], lsem.at[3]),
        pltpu.make_async_copy(x_hbm.at[1], xs.at[1], lsem.at[4]),
        pltpu.make_async_copy(m_hbm.at[1], ms.at[1], lsem.at[5]),
    ]
    for load in loads:
        load.start()

    barrier = pltpu.get_barrier_semaphore()
    for step in range(1, groups):
        pl.semaphore_signal(
            barrier, inc=1, device_id={"blk": z, "sub": peer(step)},
            device_id_type=MESH,
        )
    for step in range(groups):
        pl.semaphore_signal(
            barrier, inc=1, device_id={"blk": zprev, "sub": peer(step)}, device_id_type=MESH
        )
    loads[1].wait()
    for b in range(tiles):
        at = pl.ds(b * tile, tile)
        wh[at, :], wl[at, :] = split(w[at, :])
    loads[0].wait()
    pl.semaphore_wait(barrier, 2 * groups - 1)

    ag_slot = slots(groups)
    hp_slot = slots(1)
    a_slot = [slots(groups) for _ in range(STRATA)]
    p_slot = [slots(groups) for _ in range(STRATA)]
    c_slot = slots(groups)
    e_slot = slots(groups)
    last_slot = slots(1)
    h1_slot = slots(1)
    q_slot = slots(groups)

    for step in range(1, groups):
        send(h_hbm, h0.at[s], ag_slot + step, {"blk": z, "sub": peer(step)})
    for step in range(1, groups):
        arrived(h0.at[peer(-step)], ag_slot + step)
    send(h0, hprev, hp_slot, ahead)

    def errors(t, held):
        hh[...], hl[...] = split(held[...].reshape(groups * share_rows, rank))
        loads[2 + 2 * t].wait()
        loads[3 + 2 * t].wait()
        for b in range(tiles):
            at = pl.ds(b * tile, tile)
            predicted = dot3((wh[at, :], wl[at, :]), (hh[...], hl[...]), ((1,), (1,)))
            e = ms[t, at, :].astype(F32) * (xs[t, at, :] - predicted)
            eh[at, :], el[at, :] = split(e)
            th[:, at], tl[:, at] = split(e.T)

    def date_sums(t):
        sums = dot3((th[...], tl[...]), (wh[...], wl[...]))
        part[t] = -sums.reshape(groups, share_rows, rank)
        for step in range(1, groups):
            send(
                part.at[t, peer(step)], arecv.at[t, step], a_slot[t] + step,
                {"blk": z, "sub": peer(step)},
            )

    def pixel_grads(t):
        squares = jnp.zeros((8, 128), F32)
        for b in range(tiles):
            at = pl.ds(b * tile, tile)
            grad = ridge * w[at, :] - dot3((eh[at, :], el[at, :]), (hh[...], hl[...]))
            gw[at, :] = grad
            squares += folded_squares(grad)
        psq[t] = squares
        for step in range(1, groups):
            send(
                psq.at[t], precv.at[t, step], p_slot[t] + step,
                {"blk": z, "sub": peer(step)},
            )

    def date_share(t, held):
        value = part[t, s] + ridge * held[s]
        for step in range(1, groups):
            arrived(arecv.at[t, step], a_slot[t] + step)
            value += arecv[t, step]
        red[t] = value

    def pixel_scale(t):
        total = psq[t]
        for step in range(1, groups):
            arrived(precv.at[t, step], p_slot[t] + step)
            total += precv[t, step]
        return step_size / jnp.sqrt(whole_sum(total) / pixel_count + epsilon)

    errors(0, h0)
    date_sums(0)
    pixel_grads(0)
    date_share(0, h0)
    for i in range(chips):
        send(
            red.at[0], gath.at[s], c_slot + i, {"blk": znext, "sub": 2 * chip(i) + c}
        )
    scale = pixel_scale(0)
    for b in range(tiles):
        at = pl.ds(b * tile, tile)
        value = w[at, :] - scale * gw[at, :]
        w[at, :] = value
        wh[at, :], wl[at, :] = split(value)

    for i in range(chips):
        share = 2 * chip(-i) + c
        arrived(gath.at[share], c_slot + i)
        send(gath.at[share], gath.at[share], e_slot + i, mate)
    for i in range(chips):
        arrived(gath.at[2 * chip(-i) + 1 - c], e_slot + i)
    arrived(hprev, hp_slot)
    grads = gath[...].reshape(groups * share_rows, rank)
    scale = step_size / jnp.sqrt(whole_sum(folded_squares(grads)) / date_count + epsilon)
    h1[...] = hprev[...] - scale.reshape(1, 1, 1) * gath[...]
    send(h1.at[s], hrecv, h1_slot, ahead)

    errors(1, h1)
    date_sums(1)
    pixel_grads(1)
    date_share(1, h1)
    send(red.at[1], crecv, last_slot, ahead)
    dsq[...] = folded_squares(red[1])
    for step in range(groups):
        send(
            dsq, drecv.at[step], q_slot + step,
            {"blk": znext, "sub": peer(step)},
        )
    scale = pixel_scale(1)
    for b in range(tiles):
        at = pl.ds(b * tile, tile)
        wres[at, :] = w[at, :] - scale * gw[at, :]
    w_store = pltpu.make_async_copy(wres, w_out, lsem.at[6])
    w_store.start()
    total = jnp.zeros((8, 128), F32)
    for step in range(groups):
        arrived(drecv.at[step], q_slot + step)
        total += drecv[step]
    scale = step_size / jnp.sqrt(whole_sum(total) / date_count + epsilon)
    arrived(hrecv, h1_slot)
    arrived(crecv, last_slot)
    hres[...] = hrecv[...] - scale * crecv[...]
    h_store = pltpu.make_async_copy(hres, h_out, lsem.at[7])
    h_store.start()
    for copy in sent:
        copy.wait_send()
    w_store.wait()
    h_store.wait()
    assert used[0] <= ssem.shape[0]


def on_device(strips, groups, readings, coverage, pixel_factors, date_factors):
    rows, rank = pixel_factors.shape
    share_rows = date_factors.shape[0]
    dates = share_rows * groups
    vmem = pltpu.VMEM
    block = vmem((groups, share_rows, rank), F32)
    share = vmem((share_rows, rank), F32)
    strip = vmem((rows, rank), F32)
    slots = 8 + 9 * groups
    scratch = [
        vmem((STRATA, rows, dates), F32), vmem((STRATA, rows, dates), jnp.int32),
        strip, strip,
        vmem((rows, rank), BF16), vmem((rows, rank), BF16),
        vmem((rows, dates), BF16), vmem((rows, dates), BF16),
        vmem((dates, rows), BF16), vmem((dates, rows), BF16),
        block, block, block,
        vmem((dates, rank), BF16), vmem((dates, rank), BF16),
        block,
        vmem((STRATA, groups, share_rows, rank), F32),
        vmem((STRATA, groups, share_rows, rank), F32),
        vmem((STRATA, share_rows, rank), F32),
        share, share,
        vmem((STRATA, 8, 128), F32), vmem((STRATA, groups, 8, 128), F32),
        vmem((8, 128), F32), vmem((groups, 8, 128), F32),
        strip, share,
        pltpu.SemaphoreType.DMA((8,)),
        pltpu.SemaphoreType.DMA((slots,)),
        pltpu.SemaphoreType.DMA((slots,)),
    ]
    anywhere = pl.BlockSpec(memory_space=pl.ANY)
    return pl.pallas_call(
        functools.partial(kernel, strips, groups),
        out_shape=(
            jax.ShapeDtypeStruct((rows, rank), F32),
            jax.ShapeDtypeStruct((share_rows, rank), F32),
        ),
        in_specs=[pl.BlockSpec(memory_space=pltpu.HBM)] * 4,
        out_specs=(anywhere, anywhere),
        scratch_shapes=scratch,
        compiler_params=pltpu.CompilerParams(
            collective_id=0, has_side_effects=True, vmem_limit_bytes=53 * 1024 * 1024
        ),
    )(readings, coverage, pixel_factors, date_factors)


def solution(mesh):
    in_specs = (
        P(None, ("parts", "blk", "sub"), None),
        P(None, ("parts", "blk", "sub"), None),
        P(("parts", "blk", "sub"), None),
        P(("parts", "blk", "sub"), None),
    )
    out_specs = (P(("parts", "blk", "sub"), None), P(("parts", "blk", "sub"), None))
    return jax.shard_map(
        functools.partial(on_device, mesh.shape["blk"], mesh.shape["sub"]),
        mesh=mesh, in_specs=in_specs, out_specs=out_specs, check_vma=False,
    )
```

time: 40.5 us -> 36.5 us (0.901)
  local copies, waits for them, and re-layouts: 6.29 us -> 2.34 us
    unnamed x10 -> x4, local copies, waits for them, and re-layouts: 6.29 us -> 2.34 us
where the time goes in v2:
time: 36.5 us; the launch traced here: 36.3 us
  Pallas kernels  33.3 us (91%)
  local copies, waits for them, and re-layouts  2.34 us (6%)
  between operations  0.65 us (2%)
    pallas_call x1, Pallas kernels, on_device(): pl.pallas_call(functools.partial(kernel, strips, groups), out_shape=(jax....  33.3 us
    unnamed x4, local copies, waits for them, and re-layouts  2.34 us

profile of v2, /device:TPU:0, one launch (start us, length us, event | category | flops | bytes accessed | tf_op | source)
XLA Modules:
  0.0 36.3 jit_solution(892161614896462566)
XLA Ops:
  0.6 0.0 copy-start
  0.6 0.8 %copy-done = f32[64,256]{1,0:T(8,128)S(1)} copy-done((f32[64,256]{1,0:T(8,128)S(1)}, f32[64,256]{1,0:T(8,128)}, u32[]{:S(2)}) %copy-start) | copy-done | bytes 65560
  1.5 33.3 %shard_map.59 = (f32[768,256]{1,0:T(8,128)S(1)}, f32[64,256]{1,0:T(8,128)S(1)}) custom-call(f32[2,768,256]{2,1,0:T(8,128)} %x_hbm.1, s32[2,768,256]{2,1,0:T(8,128)} %m_hbm.1, f32[768,256]{1,0:T(8,128)} %w_hbm.1, f32[64,256]{1,0:T(8,128)S(1)} %copy-done), custom_call_target="tpu_custom_call" | custom-call | tf_op jit(solution)/shard_map/pallas_call | solution.py:275
  34.8 0.9 %copy.8 = f32[768,256]{1,0:T(8,128)} copy(f32[768,256]{1,0:T(8,128)S(1)} %get-tuple-element.4) | data formatting | bytes 1572864
  35.7 0.6 %copy.9 = f32[64,256]{1,0:T(8,128)} copy(f32[64,256]{1,0:T(8,128)S(1)} %get-tuple-element.5) | data formatting | bytes 131072
Async XLA Ops:
  0.6 0.8 %copy-start = (f32[64,256]{1,0:T(8,128)S(1)}, f32[64,256]{1,0:T(8,128)}, u32[]{:S(2)}) copy-start(f32[64,256]{1,0:T(8,128)} %h_hbm.1) | copy-start | bytes 196612

commit v3 on v2

--- a/solution.py
+++ b/solution.py
@@ -240,6 +240,17 @@
     w_store.wait()
     h_store.wait()
     assert used[0] <= ssem.shape[0]
+
+
+def hand_on(w_from, h_from, w_out, h_out, sem):
+    copies = [
+        pltpu.make_async_copy(w_from, w_out, sem.at[0]),
+        pltpu.make_async_copy(h_from, h_out, sem.at[1]),
+    ]
+    for copy in copies:
+        copy.start()
+    for copy in copies:
+        copy.wait()
 
 
 def on_device(strips, groups, readings, coverage, pixel_factors, date_factors):
@@ -272,7 +283,7 @@
         pltpu.SemaphoreType.DMA((slots,)),
     ]
     anywhere = pl.BlockSpec(memory_space=pl.ANY)
-    return pl.pallas_call(
+    strip_value, share_value = pl.pallas_call(
         functools.partial(kernel, strips, groups),
         out_shape=(
             jax.ShapeDtypeStruct((rows, rank), F32),
@@ -285,6 +296,17 @@
             collective_id=0, has_side_effects=True, vmem_limit_bytes=53 * 1024 * 1024
         ),
     )(readings, coverage, pixel_factors, date_factors)
+    return pl.pallas_call(
+        hand_on,
+        out_shape=(
+            jax.ShapeDtypeStruct((rows, rank), F32),
+            jax.ShapeDtypeStruct((share_rows, rank), F32),
+        ),
+        in_specs=[pl.BlockSpec(memory_space=pltpu.VMEM)] * 2,
+        out_specs=(anywhere, anywhere),
+        scratch_shapes=[pltpu.SemaphoreType.DMA((2,))],
+        compiler_params=pltpu.CompilerParams(vmem_limit_bytes=8 * 1024 * 1024),
+    )(strip_value, share_value)
 
 
 def solution(mesh):

time: 36.5 us -> 35.9 us (0.984)
  local copies, waits for them, and re-layouts: 2.34 us -> 0.83 us
  Pallas kernels: 33.3 us -> 34.2 us
    unnamed x4 -> x2, local copies, waits for them, and re-layouts: 2.34 us -> 0.83 us
    pallas_call x0 -> x1, Pallas kernels: none -> 0.91 us  [on_device(): pl.pallas_call(hand_on, out_shape=(jax.ShapeDtypeStruct((rows, rank), F32...]
where the time goes in v3:
time: 35.9 us; the launch traced here: 35.7 us
  Pallas kernels  34.2 us (95%)
  local copies, waits for them, and re-layouts  0.83 us (2%)
  between operations  0.65 us (2%)
    pallas_call x1, Pallas kernels, on_device(): pl.pallas_call(functools.partial(kernel, strips, groups), out_shape=(jax....  33.3 us
    pallas_call x1, Pallas kernels, on_device(): pl.pallas_call(hand_on, out_shape=(jax.ShapeDtypeStruct((rows, rank), F32...  0.91 us
    unnamed x2, local copies, waits for them, and re-layouts  0.83 us

profile of v3, /device:TPU:0, one launch (start us, length us, event | category | flops | bytes accessed | tf_op | source)
XLA Modules:
  0.0 35.7 jit_solution(8564185294483250476)
XLA Ops:
  0.6 0.0 copy-start
  0.6 0.8 %copy-done = f32[64,256]{1,0:T(8,128)S(1)} copy-done((f32[64,256]{1,0:T(8,128)S(1)}, f32[64,256]{1,0:T(8,128)}, u32[]{:S(2)}) %copy-start) | copy-done | bytes 65560
  1.5 33.3 %shard_map.59 = (f32[768,256]{1,0:T(8,128)S(1)}, f32[64,256]{1,0:T(8,128)S(1)}) custom-call(f32[2,768,256]{2,1,0:T(8,128)} %x_hbm.1, s32[2,768,256]{2,1,0:T(8,128)} %m_hbm.1, f32[768,256]{1,0:T(8,128)} %w_hbm.1, f32[64,256]{1,0:T(8,128)S(1)} %copy-done), custom_call_target="tpu_custom_call" | custom-call | tf_op jit(solution)/shard_map/pallas_call | solution.py:286
  34.8 0.9 %shard_map.60 = (f32[768,256]{1,0:T(8,128)}, f32[64,256]{1,0:T(8,128)}) custom-call(f32[768,256]{1,0:T(8,128)S(1)} %get-tuple-element.4.w_from, f32[64,256]{1,0:T(8,128)S(1)} %get-tuple-element.5.h_from), custom_call_target="tpu_custom_call" | custom-call | tf_op jit(solution)/shard_map/pallas_call | solution.py:299
Async XLA Ops:
  0.6 0.8 %copy-start = (f32[64,256]{1,0:T(8,128)S(1)}, f32[64,256]{1,0:T(8,128)}, u32[]{:S(2)}) copy-start(f32[64,256]{1,0:T(8,128)} %h_hbm.1) | copy-start | bytes 196612
